TPU v7x, 128 devices: a whole 4x4x4 slice. The times are simulated.
128 devices in a mesh: section: 2 (over core), expert: 16 (over z, y), head: 4 (over x).
Axes of the slice: x: 4, y: 4, z: 4, core: 2. Of those that a mesh axis runs over, the one named last changes fastest.
Arguments:
- inputs: bfloat16 [2, 2048, 768], P(None, 'expert'), may hold values from -6 to 6
- cotangent: bfloat16 [2, 2048, 768], P(None, 'expert'), may hold values from -6 to 6
- routes: int32 [2, 2, 2048, 2], P('section', None, 'expert'), may hold values from 0 to 31, all different within a row; in each aligned block of 128 rows (0 to 127, 128 to 255, ..., all dimensions but the last counted through in order) at most 12 rows name the same one
- attend_gain: bfloat16 [2, 768], P('section'), may hold values from 0.099609375 to 1.8984375
- query_key_value: bfloat16 [2, 3, 768, 768], P('section', None, None, 'head'), may hold values from -0.21875 to 0.21875
- attend_out: bfloat16 [2, 768, 768], P('section', 'head'), may hold values from -1.75 to 1.75
- position_bias: bfloat16 [2, 12, 32], P('section', 'head'), may hold values from -4 to 4
- mixture_gain: bfloat16 [2, 768], P('section'), may hold values from 0.099609375 to 1.8984375
- router: bfloat16 [2, 768, 32], P('section'), may hold values from -0.15625 to 0.15625
- expert_up: bfloat16 [2, 32, 768, 3072], P('section', 'expert', None, 'head'), may hold values from -0.21875 to 0.21875
- expert_down: bfloat16 [2, 32, 3072, 768], P('section', 'expert', 'head'), may hold values from -0.109375 to 0.109375
Outputs:
- section_output: bfloat16 [2, 2, 2048, 768], P('section', None, 'expert')
- input_grad: float32 [2, 2, 2048, 768], P('section', None, 'expert')
- grad_attend_gain: float32 [2, 768], P('section')
- grad_query_key_value: float32 [2, 3, 768, 768], P('section', None, None, 'head')
- grad_attend_out: float32 [2, 768, 768], P('section', 'head')
- grad_position_bias: float32 [2, 12, 32], P('section', 'head')
- grad_mixture_gain: float32 [2, 768], P('section')
- grad_router: float32 [2, 768, 32], P('section')
- grad_expert_up: float32 [2, 32, 768, 3072], P('section', 'expert', None, 'head')
- grad_expert_down: float32 [2, 32, 3072, 768], P('section', 'expert', 'head')
Inputs may be any that keep to these rules, and one draw needn't show every extreme that they name: `routes`: each token names two different experts. Among the 128 tokens of one sequence (one section, micro-batch and index of expert), no expert is named more than 12 times over both slots, and in every draw some expert is named exactly 12 times by some sequence.
All inputs are finite; a program needn't handle non-finite values.
Results may differ from a plain program's by a relative error of at most 0.028.
Values may be sent and summed in bfloat16 or wider, within the bound.
No kernel may reach another device: no remote copies, remote signals or barrier semaphores. Data moves between devices by JAX's collectives and lax.ppermute only.
A program may use at most 128 MiB of HBM per device.

v0:
```python
import jax
import jax.numpy as jnp
from jax import lax
from jax.sharding import PartitionSpec as P

HEAD_DIM = 64
EPS = 1e-06
NEG = -1e30


def passed_along(array, axis, by):
    length = lax.axis_size(axis)
    pairs = [(i, i + by) for i in range(length) if 0 <= i + by < length]
    return lax.ppermute(array, axis, pairs)


def norm_scale(values):
    return lax.rsqrt(jnp.mean(values * values, axis=-1, keepdims=True) + EPS)


def norm_back(grad_normed, values, scale, gain):
    unit = values * scale
    grad_gain = jnp.sum(grad_normed * unit, axis=0)
    grad_unit = grad_normed * gain
    grad_values = scale * (grad_unit - unit * jnp.mean(grad_unit * unit, axis=-1, keepdims=True))
    return (grad_values, grad_gain)


def position_tables(length, buckets):
    rows = lax.broadcasted_iota(jnp.int32, (length, length), 0)
    cols = lax.broadcasted_iota(jnp.int32, (length, length), 1)
    offset = rows - cols
    levels = lax.broadcasted_iota(jnp.int32, (buckets, length, length), 0)
    onehot = (jnp.clip(offset, 0, buckets - 1)[None] == levels).astype(jnp.bfloat16)
    return (offset >= 0, onehot)


def slot_targets(route_tile, experts, capacity):
    flat = route_tile.reshape(-1)
    levels = lax.broadcasted_iota(jnp.int32, (flat.shape[0], experts), 1)
    onehot = (flat[:, None] == levels).astype(jnp.int32)
    place = jnp.sum((jnp.cumsum(onehot, axis=0) - 1) * onehot, axis=1)
    return flat * capacity + place


def attend_scores(heads, table, causal, onehot):
    bias = jnp.einsum("bst,hb->hst", onehot, table, preferred_element_type=jnp.float32)
    scores = jnp.einsum("shd,thd->hst", heads[0], heads[1], preferred_element_type=jnp.float32)
    scores = scores * HEAD_DIM ** (-0.5) + bias
    return jnp.where(causal[None], scores, NEG)


def attend_forward(normed, proj_weight, out_weight, table, causal, onehot):
    length = normed.shape[0]
    local_heads = table.shape[0]
    projected = jnp.einsum(
        "sd,kde->kse", normed, proj_weight, preferred_element_type=jnp.float32
    ).astype(jnp.bfloat16)
    heads = projected.reshape(3, length, local_heads, HEAD_DIM)
    scores = attend_scores(heads, table, causal, onehot)
    top = jnp.max(scores, axis=-1, keepdims=True)
    weights = jnp.exp(scores - top)
    total = jnp.sum(weights, axis=-1, keepdims=True)
    probs = (weights / total).astype(jnp.bfloat16)
    mixed = jnp.einsum("hst,thd->shd", probs, heads[2], preferred_element_type=jnp.float32)
    mixed = mixed.reshape(length, local_heads * HEAD_DIM).astype(jnp.bfloat16)
    partial_out = jnp.dot(mixed, out_weight, preferred_element_type=jnp.float32)
    return (partial_out, (projected, mixed, top + jnp.log(total)))


def attend_backward(grad_attn, normed, proj_weight, out_weight, table, causal, onehot, saved_attn):
    projected, mixed, log_total = saved_attn
    length = normed.shape[0]
    local_heads = table.shape[0]
    heads = projected.reshape(3, length, local_heads, HEAD_DIM)
    grad_out_weight = jnp.einsum("se,sd->ed", mixed, grad_attn, preferred_element_type=jnp.float32)
    grad_mixed = jnp.einsum("sd,ed->se", grad_attn, out_weight, preferred_element_type=jnp.float32)
    grad_mixed = grad_mixed.astype(jnp.bfloat16).reshape(length, local_heads, HEAD_DIM)
    probs = jnp.exp(attend_scores(heads, table, causal, onehot) - log_total)
    grad_probs = jnp.einsum(
        "shd,thd->hst", grad_mixed, heads[2], preferred_element_type=jnp.float32
    )
    delta = jnp.sum(probs * grad_probs, axis=-1, keepdims=True)
    grad_scores = (probs * (grad_probs - delta)).astype(jnp.bfloat16)
    grad_table = jnp.einsum("bst,hst->hb", onehot, grad_scores, preferred_element_type=jnp.float32)
    factor = HEAD_DIM ** (-0.5)
    grad_query = (
        jnp.einsum("hst,thd->shd", grad_scores, heads[1], preferred_element_type=jnp.float32)
        * factor
    )
    grad_key = (
        jnp.einsum("hst,shd->thd", grad_scores, heads[0], preferred_element_type=jnp.float32)
        * factor
    )
    grad_value = jnp.einsum(
        "hst,shd->thd", probs.astype(jnp.bfloat16), grad_mixed, preferred_element_type=jnp.float32
    )
    grad_projected = (
        jnp.stack([grad_query, grad_key, grad_value])
        .reshape(3, length, local_heads * HEAD_DIM)
        .astype(jnp.bfloat16)
    )
    grad_proj_weight = jnp.einsum(
        "sd,kse->kde", normed, grad_projected, preferred_element_type=jnp.float32
    )
    grad_normed = jnp.einsum(
        "kse,kde->sd", grad_projected, proj_weight, preferred_element_type=jnp.float32
    )
    return (grad_normed, grad_proj_weight, grad_out_weight, grad_table)


def raise_hidden(arrived, up_weight):
    pre_act = jnp.einsum("erd,edf->erf", arrived, up_weight, preferred_element_type=jnp.float32)
    return (pre_act, jax.nn.gelu(pre_act).astype(jnp.bfloat16))


def gate_forward(logits, route_tile, experts):
    levels = lax.broadcasted_iota(jnp.int32, route_tile.shape + (experts,), 2)
    pick = (route_tile[:, :, None] == levels).astype(jnp.float32)
    chosen = jnp.sum(logits[:, None, :] * pick, axis=-1)
    top = jnp.max(chosen, axis=-1, keepdims=True)
    weights = jnp.exp(chosen - top)
    return (weights / jnp.sum(weights, axis=-1, keepdims=True), pick)


def layer_forward(layer_in, route_tile, params, tables):
    gain_a, proj_weight, out_weight, table, gain_m, router_weight, up_weight, down_weight = params
    causal, onehot = tables
    values = layer_in.astype(jnp.float32)
    length, width = values.shape
    experts = router_weight.shape[1]
    local_experts = up_weight.shape[0]
    capacity = 3 * length // experts
    scale_a = norm_scale(values)
    normed_a = (values * scale_a * gain_a).astype(jnp.bfloat16)
    partial_attn, saved_attn = attend_forward(
        normed_a, proj_weight, out_weight, table, causal, onehot
    )
    attended = lax.psum(partial_attn, "head")
    middle = values + attended
    scale_m = norm_scale(middle)
    normed_m = (middle * scale_m * gain_m).astype(jnp.bfloat16)
    logits = jnp.dot(normed_m, router_weight, preferred_element_type=jnp.float32)
    gates, pick = gate_forward(logits, route_tile, experts)
    target = slot_targets(route_tile, experts, capacity)
    buffer = (
        jnp.zeros((experts * capacity, width), jnp.bfloat16)
        .at[target]
        .set(jnp.repeat(normed_m, 2, axis=0))
    )
    arrived = lax.all_to_all(
        buffer.reshape(experts, 1, capacity, width),
        "expert",
        split_axis=0,
        concat_axis=1,
        tiled=True,
    )
    arrived = arrived.reshape(local_experts, -1, width)
    pre_act, hidden = raise_hidden(arrived, up_weight)
    partial_rows = jnp.einsum(
        "erf,efd->erd", hidden, down_weight, preferred_element_type=jnp.float32
    )
    returned = lax.all_to_all(
        partial_rows.reshape(local_experts, -1, capacity, width).astype(jnp.bfloat16),
        "expert",
        split_axis=1,
        concat_axis=0,
        tiled=True,
    ).astype(jnp.float32)
    slot_part = returned.reshape(experts * capacity, width)[target].reshape(length, 2, width)
    slot_out = lax.psum(slot_part.astype(jnp.bfloat16), "head").astype(jnp.float32)
    layer_out = middle + jnp.sum(gates[:, :, None] * slot_out, axis=1)
    owner_saved = (buffer,)
    saved = (
        values,
        scale_a,
        normed_a,
        saved_attn,
        middle,
        scale_m,
        normed_m,
        gates,
        pick,
        target,
        slot_out,
        owner_saved,
    )
    return (layer_out, saved)


def layer_backward(grad_out, saved, params, tables):
    gain_a, proj_weight, out_weight, table, gain_m, router_weight, up_weight, down_weight = params
    causal, onehot = tables
    (
        values,
        scale_a,
        normed_a,
        saved_attn,
        middle,
        scale_m,
        normed_m,
        gates,
        pick,
        target,
        slot_out,
        owner_saved,
    ) = saved
    length, width = values.shape
    experts = router_weight.shape[1]
    local_experts = up_weight.shape[0]
    capacity = 3 * length // experts
    grad_slots = (gates[:, :, None] * grad_out[:, None, :]).astype(jnp.bfloat16)
    grad_gates = jnp.sum(grad_out[:, None, :] * slot_out, axis=-1)
    grad_buffer = (
        jnp.zeros((experts * capacity, width), jnp.bfloat16)
        .at[target]
        .set(grad_slots.reshape(2 * length, width))
    )
    grad_buffer = grad_buffer.reshape(experts, 1, capacity, width)
    row_buffer = owner_saved[0].reshape(experts, 1, capacity, width)
    grad_arrived, arrived = (
        lax.all_to_all(grad_buffer, "expert", split_axis=0, concat_axis=1, tiled=True),
        lax.all_to_all(row_buffer, "expert", split_axis=0, concat_axis=1, tiled=True),
    )
    arrived = arrived.reshape(local_experts, -1, width)
    pre_act, hidden = raise_hidden(arrived, up_weight)
    grad_arrived = grad_arrived.reshape(local_experts, -1, width)
    grad_hidden = jnp.einsum(
        "erd,efd->erf", grad_arrived, down_weight, preferred_element_type=jnp.float32
    )
    unused, gelu_back = jax.vjp(jax.nn.gelu, pre_act)
    grad_pre = gelu_back(grad_hidden)[0].astype(jnp.bfloat16)
    grad_down = jnp.einsum("erf,erd->efd", hidden, grad_arrived, preferred_element_type=jnp.float32)
    grad_up = jnp.einsum("erd,erf->edf", arrived, grad_pre, preferred_element_type=jnp.float32)
    grad_rows = jnp.einsum("erf,edf->erd", grad_pre, up_weight, preferred_element_type=jnp.float32)
    returned = lax.all_to_all(
        grad_rows.reshape(local_experts, -1, capacity, width).astype(jnp.bfloat16),
        "expert",
        split_axis=1,
        concat_axis=0,
        tiled=True,
    ).astype(jnp.float32)
    grad_slot_rows = returned.reshape(experts * capacity, width)[target].reshape(length, 2, width)
    grad_normed_m = lax.psum(jnp.sum(grad_slot_rows, axis=1).astype(jnp.bfloat16), "head").astype(
        jnp.float32
    )
    grad_chosen = gates * (grad_gates - jnp.sum(gates * grad_gates, axis=-1, keepdims=True))
    grad_logits = jnp.sum(grad_chosen[:, :, None] * pick, axis=1).astype(jnp.bfloat16)
    grad_router = jnp.einsum("sd,se->de", normed_m, grad_logits, preferred_element_type=jnp.float32)
    grad_normed_m = grad_normed_m + jnp.einsum(
        "se,de->sd", grad_logits, router_weight, preferred_element_type=jnp.float32
    )
    grad_middle, grad_gain_m = norm_back(grad_normed_m, middle, scale_m, gain_m)
    grad_middle = grad_middle + grad_out
    grad_normed_a, grad_proj_weight, grad_out_weight, grad_table = attend_backward(
        grad_middle.astype(jnp.bfloat16),
        normed_a,
        proj_weight,
        out_weight,
        table,
        causal,
        onehot,
        saved_attn,
    )
    grad_normed_a = lax.psum(grad_normed_a.astype(jnp.bfloat16), "head").astype(jnp.float32)
    grad_values, grad_gain_a = norm_back(grad_normed_a, values, scale_a, gain_a)
    shared = (grad_gain_a, grad_proj_weight, grad_out_weight, grad_table, grad_gain_m, grad_router)
    return (grad_values + grad_middle, shared, (grad_up, grad_down))


def on_device(
    inputs,
    cotangent,
    routes,
    attend_gain,
    query_key_value,
    attend_out,
    position_bias,
    mixture_gain,
    router,
    expert_up,
    expert_down,
):
    micro = inputs.shape[0]
    length = inputs.shape[1]
    params = (
        attend_gain[0].astype(jnp.float32),
        query_key_value[0],
        attend_out[0],
        position_bias[0],
        mixture_gain[0].astype(jnp.float32),
        router[0],
        expert_up[0],
        expert_down[0],
    )
    tables = position_tables(length, position_bias.shape[2])
    first = lax.axis_index("section") == 0
    received = jnp.zeros((length, inputs.shape[2]), jnp.bfloat16)
    outputs = []
    caches = []
    for tick in range(micro + 1):
        layer_in = jnp.where(first, inputs[min(tick, micro - 1)], received)
        route_tile = jnp.where(first, routes[0, min(tick, micro - 1)], routes[0, max(tick - 1, 0)])
        layer_out, saved = layer_forward(layer_in, route_tile, params, tables)
        layer_low = layer_out.astype(jnp.bfloat16)
        outputs.append(layer_low)
        caches.append(saved)
        if tick < micro:
            received = passed_along(layer_low, "section", 1)
    section_output = jnp.stack(
        [jnp.where(first, outputs[index], outputs[index + 1]) for index in range(micro)]
    )[None]
    grad_received = jnp.zeros_like(received)
    shared_total = None
    owned_total = None
    grad_list = []
    for tick in range(micro + 1):
        late = cotangent[min(tick, micro - 1)].astype(jnp.float32)
        if tick == micro:
            late = jnp.zeros_like(late)
        grad_out = jnp.where(first, grad_received.astype(jnp.float32), late)
        saved = jax.tree.map(
            lambda early, later: jnp.where(first, early, later),
            caches[max(tick - 1, 0)],
            caches[min(tick + 1, micro)],
        )
        grad_in, shared, owned = layer_backward(grad_out, saved, params, tables)
        if shared_total is None:
            shared_total = shared
            owned_total = owned
        else:
            shared_total = jax.tree.map(lambda total, extra: total + extra, shared_total, shared)
            owned_total = jax.tree.map(lambda total, extra: total + extra, owned_total, owned)
        grad_list.append(grad_in)
        if tick < micro:
            grad_received = passed_along(grad_in.astype(jnp.bfloat16), "section", -1)
    gain_a, proj_part, out_part, table_part, gain_m, router_part = shared_total
    shared_total = (
        lax.psum(gain_a.astype(jnp.bfloat16), "expert").astype(jnp.float32),
        lax.psum(proj_part.astype(jnp.bfloat16), "expert").astype(jnp.float32),
        lax.psum(out_part.astype(jnp.bfloat16), "expert").astype(jnp.float32),
        lax.psum(table_part.astype(jnp.bfloat16), "expert").astype(jnp.float32),
        lax.psum(gain_m.astype(jnp.bfloat16), "expert").astype(jnp.float32),
        lax.psum(router_part.astype(jnp.bfloat16), "expert").astype(jnp.float32),
    )
    input_grad = jnp.stack(
        [jnp.where(first, grad_list[index + 1], grad_list[index]) for index in range(micro)]
    )[None]
    grad_gain_a, grad_proj, grad_out_weight, grad_table, grad_gain_m, grad_router = shared_total
    grad_up, grad_down = owned_total
    return (
        section_output,
        input_grad,
        grad_gain_a[None],
        grad_proj[None],
        grad_out_weight[None],
        grad_table[None],
        grad_gain_m[None],
        grad_router[None],
        grad_up[None],
        grad_down[None],
    )


def solution(mesh):
    return jax.shard_map(
        on_device,
        mesh=mesh,
        in_specs=(
            P(None, "expert", None),
            P(None, "expert", None),
            P("section", None, "expert", None),
            P("section", None),
            P("section", None, None, "head"),
            P("section", "head", None),
            P("section", "head", None),
            P("section", None),
            P("section", None, None),
            P("section", "expert", None, "head"),
            P("section", "expert", "head", None),
        ),
        out_specs=(
            P("section", None, "expert", None),
            P("section", None, "expert", None),
            P("section", None),
            P("section", None, None, "head"),
            P("section", "head", None),
            P("section", "head", None),
            P("section", None),
            P("section", None, None),
            P("section", "expert", None, "head"),
            P("section", "expert", "head", None),
        ),
        check_vma=False,
    )
```

profile of v0, /device:TPU:0, one launch (start us, length us, event | category | flops | bytes accessed | tf_op | source)
XLA Modules:
  0.0 950.1 jit_solution(12501314368429168360)
XLA Ops:
  22.1 39.1 %all-reduce.16.cloned.1.call-done = f32[128,768]{1,0:T(8,128)} async-done(((f32[128,768]{1,0:T(8,128)}), f32[128,768]{1,0:T(8,128)}) %all-reduce.16.cloned.1.call-update) | async-done | bytes 393232 | tf_op jit(solution)/shard_map/psum | solution.py:139
  68.0 19.2 %all_to_all.189 = bf16[32,1,12,768]{3,2,1,0:T(8,128)(2,1)S(1)} all-to-all(bf16[32,1,12,768]{3,2,1,0:T(8,128)(2,1)} %bitcast.600), channel_id=1, replica_groups=mesh['section'=2,'expert'=16,'head'=4] {'expert'}, dimensions={0} | all-to-all | bytes 1179648 | tf_op jit(solution)/shard_map/all_to_all | solution.py:151
  88.1 3.7 fusion.44
  94.4 3.6 all-to-all-start.1
  98.2 10.2 %all-to-all-done.1 = bf16[2,16,12,768]{3,0,2,1:T(2,128)(2,1)S(1)} async-done(((bf16[2,16,12,768]{3,0,2,1:T(2,128)(2,1)}), bf16[2,16,12,768]{3,0,2,1:T(2,128)(2,1)S(1)}, u32[]{:S(2)}, u32[]{:S(2)}) %all-to-all-start.1) | async-done | bytes 589856 | tf_op jit(solution)/shard_map/all_to_all | solution.py:163
  114.5 38.0 %all-reduce.18.cloned.1.call-done = bf16[128,2,768]{2,1,0:T(2,128)(2,1)} async-done(((bf16[128,2,768]{2,1,0:T(2,128)(2,1)}), bf16[128,2,768]{2,1,0:T(2,128)(2,1)}) %all-reduce.18.cloned.1.call-update) | async-done | bytes 393232 | tf_op jit(solution)/shard_map/psum | solution.py:171
  164.4 40.4 %all-reduce.20.cloned.1.call-done = f32[128,768]{1,0:T(8,128)} async-done(((f32[128,768]{1,0:T(8,128)}), f32[128,768]{1,0:T(8,128)}) %all-reduce.20.cloned.1.call-update) | async-done | bytes 393232 | tf_op jit(solution)/shard_map/psum | solution.py:139
  214.6 7.0 all-to-all-start.7
  225.1 8.9 all-to-all-done.7
  234.0 4.3 all-to-all-start.2
  244.1 5.9 all-to-all-done.2
  250.1 4.3 all-to-all-start.6
  259.3 3.8 fusion.47
  266.0 6.9 all-to-all-start.3
  284.2 5.0 all-to-all-start.8
  310.8 3.0 fusion.217
  313.8 3.1 fusion.176
  317.0 37.1 %all-reduce.36.cloned.1.call-done = (bf16[128,768]{1,0:T(8,128)(2,1)}, bf16[128,2,768]{2,1,0:T(2,128)(2,1)}) async-done(((bf16[128,768]{1,0:T(8,128)(2,1)}, bf16[128,2,768]{2,1,0:T(2,128)(2,1)}), (bf16[128,768]{1,0:T(8,128)(2,1)}, bf16[128,2,768]{2,1,0:T(2,128)(2,1)})) %all-reduce.36.cloned.1.call-update) | async-done | bytes 589840 | tf_op jit(solution)/shard_map/psum | solution.py:244
  354.1 4.0 fusion.170
  369.2 38.2 %all-reduce.24.cloned.1.call-done = bf16[128,768]{1,0:T(8,128)(2,1)} async-done(((bf16[128,768]{1,0:T(8,128)(2,1)}), bf16[128,768]{1,0:T(8,128)(2,1)}) %all-reduce.24.cloned.1.call-update) | async-done | bytes 196624 | tf_op jit(solution)/shard_map/psum | solution.py:265
  420.9 37.7 %all-reduce.22.cloned.1.call-done = f32[128,768]{1,0:T(8,128)} async-done(((f32[128,768]{1,0:T(8,128)}), f32[128,768]{1,0:T(8,128)}) %all-reduce.22.cloned.1.call-update) | async-done | bytes 393232 | tf_op jit(solution)/shard_map/psum | solution.py:139
  464.9 2.9 scatter_custom_fusion.2
  472.0 7.2 all-to-all-start.13
  486.3 5.2 all-to-all-done.13
  491.6 4.5 all-to-all-start.4
  504.0 6.3 all-to-all-done.4
  510.3 4.3 all-to-all-start.10
  520.0 7.7 all-to-all-done.10
  527.6 4.3 all-to-all-start.9
  538.2 2.9 fusion.50
  544.7 7.4 all-to-all-start.5
  562.6 4.8 all-to-all-start.11
  567.5 3.0 fusion.212
  591.9 3.1 fusion.177
  595.1 37.2 %all-reduce.34.cloned.1.call-done = (bf16[128,768]{1,0:T(8,128)(2,1)}, bf16[128,2,768]{2,1,0:T(2,128)(2,1)}) async-done(((bf16[128,768]{1,0:T(8,128)(2,1)}, bf16[128,2,768]{2,1,0:T(2,128)(2,1)}), (bf16[128,768]{1,0:T(8,128)(2,1)}, bf16[128,2,768]{2,1,0:T(2,128)(2,1)})) %all-reduce.34.cloned.1.call-update) | async-done | bytes 589840 | tf_op jit(solution)/shard_map/psum | solution.py:244
  649.4 39.0 %all-reduce.26.cloned.1.call-done = bf16[128,768]{1,0:T(8,128)(2,1)} async-done(((bf16[128,768]{1,0:T(8,128)(2,1)}), bf16[128,768]{1,0:T(8,128)(2,1)}) %all-reduce.26.cloned.1.call-update) | async-done | bytes 196624 | tf_op jit(solution)/shard_map/psum | solution.py:265
  707.3 7.2 all-to-all-start.12
  717.3 11.9 %all-to-all-done.12 = bf16[32,1,12,768]{3,2,1,0:T(8,128)(2,1)} async-done(((bf16[32,1,12,768]{3,2,1,0:T(8,128)(2,1)}), bf16[32,1,12,768]{3,2,1,0:T(8,128)(2,1)}, u32[]{:S(2)}, u32[]{:S(2)}) %all-to-all-start.12) | async-done | bytes 589856 | tf_op jit(solution)/shard_map/all_to_all | solution.py:222
  731.4 3.1 fusion.74
  736.9 4.2 all-to-all-start.14
  741.2 7.2 add_bitcast_fusion
  748.5 4.2 all-to-all-done.14
  762.5 7.3 add_bitcast_fusion.1
  769.7 30.9 %all-reduce.28.cloned.1.call-done = bf16[128,768]{1,0:T(8,128)(2,1)} async-done(((bf16[128,768]{1,0:T(8,128)(2,1)}), bf16[128,768]{1,0:T(8,128)(2,1)}) %all-reduce.28.cloned.1.call-update) | async-done | bytes 196624 | tf_op jit(solution)/shard_map/psum | solution.py:244
  806.6 3.5 fusion.34
  816.8 31.7 %all-reduce.30.cloned.1.call-done = bf16[128,768]{1,0:T(8,128)(2,1)} async-done(((bf16[128,768]{1,0:T(8,128)(2,1)}), bf16[128,768]{1,0:T(8,128)(2,1)}) %all-reduce.30.cloned.1.call-update) | async-done | bytes 196624 | tf_op jit(solution)/shard_map/psum | solution.py:265
  850.9 75.9 %all-reduce = (bf16[1,3,32]{2,1,0:T(4,128)(2,1)}, bf16[1,768]{1,0:T(2,128)(2,1)}, bf16[1,768]{1,0:T(2,128)(2,1)S(1)}, bf16[1,768,32]{1,2,0:T(8,128)(2,1)}) all-reduce(bf16[1,3,32]{2,1,0:T(4,128)(2,1)} %fusion.153, bf16[1,768]{1,0:T(2,128)(2,1)S(1)} %broadcast_in_dim.93, ...), channel_id=1, replica_groups=mesh['section'=2,'expert'=16,'head'=4] {'expert'}, use_global_device_ids=true, to_apply=%region_78.79 | all-reduce | flops 26208 | bytes 104832 | tf_op jit(solution)/shard_map/psum | solution.py:342
  934.2 6.0 all-reduce.32.cloned.1.call-done
  (777 shorter events, 276.6 us)
Async XLA Ops:
  7.2 80.9 %copy-start = (bf16[1,2,768,768]{3,2,1,0:T(8,128)(2,1)S(1)}, bf16[1,2,768,768]{3,2,1,0:T(8,128)(2,1)}, u32[]{:S(2)}) copy-start(bf16[1,2,768,768]{3,2,1,0:T(8,128)(2,1)} %param.20) | copy-start | bytes 7077892
  7.2 54.1 %all-reduce.16.cloned.1.call-start = ((), (), s32[]{:S(2)}) async-start(), calls=%async_computation.15 | async-start | bytes 786432 | tf_op jit(solution)/shard_map/psum | solution.py:139
  8.6 149.8 %copy-start.203 = (f32[128]{0:T(128)}, f32[128]{0:T(128)S(1)}, u32[]{:S(2)}) copy-start(f32[128]{0:T(128)S(1)} %fusion.245) | copy-start | bytes 1540
  9.3 149.7 %copy-start.103 = (f32[768]{0:T(1024)}, f32[768]{0:T(1024)S(1)}, u32[]{:S(2)}) copy-start(f32[768]{0:T(1024)S(1)} %convert_reduce_fusion.1) | copy-start | bytes 9220
  15.5 45.8 %copy-start.14 = (bf16[2,128,768]{2,1,0:T(8,128)(2,1)S(1)}, bf16[2,128,768]{2,1,0:T(8,128)(2,1)}, u32[]{:S(2)}) copy-start(bf16[2,128,768]{2,1,0:T(8,128)(2,1)} %param.11) | copy-start | bytes 1179652
  17.1 96.1 %copy-start.171 = (s32[128,2]{0,1:T(2,128)}, s32[128,2]{0,1:T(2,128)S(1)}, u32[]{:S(2)}) copy-start(s32[128,2]{0,1:T(2,128)S(1)} %get-tuple-element.130) | copy-start | bytes 3076
  20.6 185.8 %copy-start.119 = (f32[768]{0:T(1024)}, f32[768]{0:T(1024)S(1)}, u32[]{:S(2)}) copy-start(f32[768]{0:T(1024)S(1)} %convert_reduce_fusion) | copy-start | bytes 9220
  62.4 143.5 %copy-start.205 = (f32[128]{0:T(128)}, f32[128]{0:T(128)S(1)}, u32[]{:S(2)}) copy-start(f32[128]{0:T(128)S(1)} %multiply_reduce_fusion.8) | copy-start | bytes 1540
  94.4 14.0 %all-to-all-start.1 = ((bf16[2,16,12,768]{3,0,2,1:T(2,128)(2,1)}), bf16[2,16,12,768]{3,0,2,1:T(2,128)(2,1)S(1)}, u32[]{:S(2)}, u32[]{:S(2)}) async-start(bf16[2,16,12,768]{3,0,2,1:T(2,128)(2,1)} %bitcast.613), calls=%async_computation.1 | async-start | bytes 1179648 | tf_op jit(solution)/shard_map/all_to_all | solution.py:163
  97.9 54.5 %all-reduce.18.cloned.1.call-start = ((), (), s32[]{:S(2)}) async-start(), calls=%async_computation.16 | async-start | bytes 786432 | tf_op jit(solution)/shard_map/psum | solution.py:171
  113.2 91.6 %all-reduce.20.cloned.1.call-start = ((), (), s32[]{:S(2)}) async-start(), calls=%async_computation.17 | async-start | bytes 786432 | tf_op jit(solution)/shard_map/psum | solution.py:139
  114.5 44.6 %copy-start.9 = (bf16[1,3,768,192]{2,3,1,0:T(8,128)(2,1)S(1)}, bf16[1,3,768,192]{2,3,1,0:T(8,128)(2,1)}, u32[]{:S(2)}) copy-start(bf16[1,3,768,192]{2,3,1,0:T(8,128)(2,1)} %param.15) | copy-start | bytes 2654212
  155.7 2.5 collective-permute-start
  158.4 48.0 %copy-start.1 = (bf16[128,768]{1,0:T(8,128)(2,1)}, bf16[128,768]{1,0:T(8,128)(2,1)S(1)}, u32[]{:S(2)}) copy-start(bf16[128,768]{1,0:T(8,128)(2,1)S(1)} %get-tuple-element.96) | copy-start | bytes 589828
  214.6 19.4 %all-to-all-start.7 = ((bf16[32,1,12,768]{3,2,1,0:T(8,128)(2,1)}), bf16[32,1,12,768]{3,2,1,0:T(8,128)(2,1)}, u32[]{:S(2)}, u32[]{:S(2)}) async-start(bf16[32,1,12,768]{3,2,1,0:T(8,128)(2,1)} %bitcast.598), calls=%async_computation.7 | async-start | bytes 1572864 | tf_op jit(solution)/shard_map/all_to_all | solution.py:223
  234.0 16.1 %all-to-all-start.2 = ((bf16[32,1,12,768]{3,2,1,0:T(8,128)(2,1)}), bf16[32,1,12,768]{3,2,1,0:T(8,128)(2,1)}, u32[]{:S(2)}, u32[]{:S(2)}) async-start(bf16[32,1,12,768]{3,2,1,0:T(8,128)(2,1)} %bitcast.596), calls=%async_computation.2 | async-start | bytes 1572864 | tf_op jit(solution)/shard_map/all_to_all | solution.py:151
  250.1 15.9 %all-to-all-start.6 = ((bf16[32,1,12,768]{3,2,1,0:T(8,128)(2,1)}), bf16[32,1,12,768]{3,2,1,0:T(8,128)(2,1)}, u32[]{:S(2)}, u32[]{:S(2)}) async-start(bf16[32,1,12,768]{3,2,1,0:T(8,128)(2,1)} %bitcast.80), calls=%async_computation.6 | async-start | bytes 1572864 | tf_op jit(solution)/shard_map/all_to_all | solution.py:222
  266.0 17.4 %all-to-all-start.3 = ((bf16[2,16,12,768]{3,0,2,1:T(2,128)(2,1)}), bf16[2,16,12,768]{3,0,2,1:T(2,128)(2,1)S(1)}, u32[]{:S(2)}, u32[]{:S(2)}) async-start(bf16[2,16,12,768]{3,0,2,1:T(2,128)(2,1)} %bitcast.611), calls=%async_computation.3 | async-start | bytes 1179648 | tf_op jit(solution)/shard_map/all_to_all | solution.py:163
  284.2 15.4 %all-to-all-start.8 = ((bf16[2,16,12,768]{3,0,2,1:T(2,128)(2,1)}), bf16[2,16,12,768]{3,0,2,1:T(2,128)(2,1)S(1)}, u32[]{:S(2)}, u32[]{:S(2)}) async-start(bf16[2,16,12,768]{3,0,2,1:T(2,128)(2,1)} %bitcast.88), calls=%async_computation.8 | async-start | bytes 1179648 | tf_op jit(solution)/shard_map/all_to_all | solution.py:236
  289.1 64.9 %all-reduce.36.cloned.1.call-start = ((), (), s32[]{:S(2)}) async-start(), calls=%async_computation.25 | async-start | bytes 1179648 | tf_op jit(solution)/shard_map/psum | solution.py:244
  310.3 97.2 %all-reduce.24.cloned.1.call-start = ((), (), s32[]{:S(2)}) async-start(), calls=%async_computation.19 | async-start | bytes 393216 | tf_op jit(solution)/shard_map/psum | solution.py:265
  316.9 42.8 %copy-start.2 = (bf16[128,768]{1,0:T(8,128)(2,1)S(1)}, bf16[128,768]{1,0:T(8,128)(2,1)}, u32[]{:S(2)}) copy-start(bf16[128,768]{1,0:T(8,128)(2,1)} %copy-done.1) | copy-start | bytes 589828
  316.9 42.8 %copy-start.16 = (bf16[2,128,768]{2,1,0:T(8,128)(2,1)S(1)}, bf16[2,128,768]{2,1,0:T(8,128)(2,1)}, u32[]{:S(2)}) copy-start(bf16[2,128,768]{2,1,0:T(8,128)(2,1)} %param.11) | copy-start | bytes 1179652
  316.9 42.8 %copy-start.24 = (f32[128,768]{1,0:T(8,128)S(1)}, f32[128,768]{1,0:T(8,128)}, u32[]{:S(2)}) copy-start(f32[128,768]{1,0:T(8,128)} %all-reduce.16.cloned.1.call-done) | copy-start | bytes 1179652
  316.9 42.8 %copy-start.82 = (bf16[1,768,32]{1,2,0:T(8,128)(2,1)S(1)}, bf16[1,768,32]{1,2,0:T(8,128)(2,1)}, u32[]{:S(2)}) copy-start(bf16[1,768,32]{1,2,0:T(8,128)(2,1)} %param.19) | copy-start | bytes 147460
  316.9 42.8 %copy-start.120 = (f32[768]{0:T(1024)S(1)}, f32[768]{0:T(1024)}, u32[]{:S(2)}) copy-start(f32[768]{0:T(1024)} %copy-done.119) | copy-start | bytes 9220
  316.9 42.8 %copy-start.201 = (f32[128]{0:T(128)S(1)}, f32[128]{0:T(128)}, u32[]{:S(2)}) copy-start(f32[128]{0:T(128)} %get-tuple-element.144) | copy-start | bytes 1540
  365.2 93.4 %all-reduce.22.cloned.1.call-start = ((), (), s32[]{:S(2)}) async-start(), calls=%async_computation.18 | async-start | bytes 786432 | tf_op jit(solution)/shard_map/psum | solution.py:139
  367.3 42.1 %collective-permute-start.1 = (bf16[128,768]{1,0:T(8,128)(2,1)S(1)}, bf16[128,768]{1,0:T(8,128)(2,1)}, u32[]{:S(2)}, u32[]{:S(2)}) collective-permute-start(bf16[128,768]{1,0:T(8,128)(2,1)S(1)} %get-tuple-element.84), channel_id=1, source_target_pairs={{0,64},{1,65},{2,66},{3,67},{4,68},{5,69},{6,70},{7,71},{8,72},{9,... | collective-permute-start | bytes 589832 | tf_op jit(solution)/shard_map/ppermute | solution.py:14
  411.4 48.9 %copy-start.5 = (bf16[128,768]{1,0:T(8,128)(2,1)}, bf16[128,768]{1,0:T(8,128)(2,1)S(1)}, u32[]{:S(2)}) copy-start(bf16[128,768]{1,0:T(8,128)(2,1)S(1)} %get-tuple-element.92) | copy-start | bytes 589828
  472.0 19.5 %all-to-all-start.13 = ((bf16[32,1,12,768]{3,2,1,0:T(8,128)(2,1)}), bf16[32,1,12,768]{3,2,1,0:T(8,128)(2,1)}, u32[]{:S(2)}, u32[]{:S(2)}) async-start(bf16[32,1,12,768]{3,2,1,0:T(8,128)(2,1)} %bitcast.129), calls=%async_computation.13 | async-start | bytes 1572864 | tf_op jit(solution)/shard_map/all_to_all | solution.py:223
  481.3 16.1 %collective-permute-start.2 = (bf16[128,768]{1,0:T(8,128)(2,1)}, bf16[128,768]{1,0:T(8,128)(2,1)}, u32[]{:S(2)}, u32[]{:S(2)}) collective-permute-start(bf16[128,768]{1,0:T(8,128)(2,1)} %get-tuple-element.99), channel_id=1, source_target_pairs={{64,0},{65,1},{66,2},{67,3},{68,4},{69,5},{70,6},{71,7},{72,8},{73... | collective-permute-start | bytes 589832 | tf_op jit(solution)/shard_map/ppermute | solution.py:14
  491.6 18.7 %all-to-all-start.4 = ((bf16[32,1,12,768]{3,2,1,0:T(8,128)(2,1)}), bf16[32,1,12,768]{3,2,1,0:T(8,128)(2,1)}, u32[]{:S(2)}, u32[]{:S(2)}) async-start(bf16[32,1,12,768]{3,2,1,0:T(8,128)(2,1)} %bitcast.595), calls=%async_computation.4 | async-start | bytes 1572864 | tf_op jit(solution)/shard_map/all_to_all | solution.py:151
  510.3 17.3 %all-to-all-start.10 = ((bf16[32,1,12,768]{3,2,1,0:T(8,128)(2,1)}), bf16[32,1,12,768]{3,2,1,0:T(8,128)(2,1)}, u32[]{:S(2)}, u32[]{:S(2)}) async-start(bf16[32,1,12,768]{3,2,1,0:T(8,128)(2,1)} %bitcast.594), calls=%async_computation.10 | async-start | bytes 1572864 | tf_op jit(solution)/shard_map/all_to_all | solution.py:223
  527.6 17.1 %all-to-all-start.9 = ((bf16[32,1,12,768]{3,2,1,0:T(8,128)(2,1)}), bf16[32,1,12,768]{3,2,1,0:T(8,128)(2,1)}, u32[]{:S(2)}, u32[]{:S(2)}) async-start(bf16[32,1,12,768]{3,2,1,0:T(8,128)(2,1)} %bitcast.101), calls=%async_computation.9 | async-start | bytes 1572864 | tf_op jit(solution)/shard_map/all_to_all | solution.py:222
  544.7 17.9 %all-to-all-start.5 = ((bf16[2,16,12,768]{3,0,2,1:T(2,128)(2,1)}), bf16[2,16,12,768]{3,0,2,1:T(2,128)(2,1)}, u32[]{:S(2)}, u32[]{:S(2)}) async-start(bf16[2,16,12,768]{3,0,2,1:T(2,128)(2,1)} %bitcast.68), calls=%async_computation.5 | async-start | bytes 1179648 | tf_op jit(solution)/shard_map/all_to_all | solution.py:163
  562.6 15.4 %all-to-all-start.11 = ((bf16[2,16,12,768]{3,0,2,1:T(2,128)(2,1)}), bf16[2,16,12,768]{3,0,2,1:T(2,128)(2,1)}, u32[]{:S(2)}, u32[]{:S(2)}) async-start(bf16[2,16,12,768]{3,0,2,1:T(2,128)(2,1)} %bitcast.610), calls=%async_computation.11 | async-start | bytes 1179648 | tf_op jit(solution)/shard_map/all_to_all | solution.py:236
  567.4 64.8 %all-reduce.34.cloned.1.call-start = ((), (), s32[]{:S(2)}) async-start(), calls=%async_computation.24 | async-start | bytes 1179648 | tf_op jit(solution)/shard_map/psum | solution.py:244
  589.7 98.6 %all-reduce.26.cloned.1.call-start = ((), (), s32[]{:S(2)}) async-start(), calls=%async_computation.20 | async-start | bytes 393216 | tf_op jit(solution)/shard_map/psum | solution.py:265
  646.1 44.0 %copy-start.3 = (bf16[128,768]{1,0:T(8,128)(2,1)S(1)}, bf16[128,768]{1,0:T(8,128)(2,1)}, u32[]{:S(2)}) copy-start(bf16[128,768]{1,0:T(8,128)(2,1)} %copy-done.1) | copy-start | bytes 589828
  646.2 44.0 %copy-start.31 = (f32[128,768]{1,0:T(8,128)S(1)}, f32[128,768]{1,0:T(8,128)}, u32[]{:S(2)}) copy-start(f32[128,768]{1,0:T(8,128)} %copy-done.29) | copy-start | bytes 1179652
  693.2 3.3 collective-permute-start.3
  707.3 22.0 %all-to-all-start.12 = ((bf16[32,1,12,768]{3,2,1,0:T(8,128)(2,1)}), bf16[32,1,12,768]{3,2,1,0:T(8,128)(2,1)}, u32[]{:S(2)}, u32[]{:S(2)}) async-start(bf16[32,1,12,768]{3,2,1,0:T(8,128)(2,1)} %bitcast.597), calls=%async_computation.12 | async-start | bytes 1572864 | tf_op jit(solution)/shard_map/all_to_all | solution.py:222
  736.9 15.8 %all-to-all-start.14 = ((bf16[2,16,12,768]{3,0,2,1:T(2,128)(2,1)}), bf16[2,16,12,768]{3,0,2,1:T(2,128)(2,1)}, u32[]{:S(2)}, u32[]{:S(2)}) async-start(bf16[2,16,12,768]{3,0,2,1:T(2,128)(2,1)} %bitcast.612), calls=%async_computation.14 | async-start | bytes 1179648 | tf_op jit(solution)/shard_map/all_to_all | solution.py:236
  741.2 59.4 %all-reduce.28.cloned.1.call-start = ((), (), s32[]{:S(2)}) async-start(), calls=%async_computation.21 | async-start | bytes 393216 | tf_op jit(solution)/shard_map/psum | solution.py:244
  762.4 86.1 %all-reduce.30.cloned.1.call-start = ((), (), s32[]{:S(2)}) async-start(), calls=%async_computation.22 | async-start | bytes 393216 | tf_op jit(solution)/shard_map/psum | solution.py:265
  806.5 133.6 %all-reduce.32.cloned.1.call-start = ((), (), s32[]{:S(2)}) async-start(), calls=%async_computation.23 | async-start | bytes 2359296 | tf_op jit(solution)/shard_map/psum | solution.py:340
  811.1 121.0 %copy-start.65 = (f32[128,768]{1,0:T(8,128)S(1)}, f32[128,768]{1,0:T(8,128)}, u32[]{:S(2)}) copy-start(f32[128,768]{1,0:T(8,128)} %copy-done.64) | copy-start | bytes 1179652
  (204 other events, 1802.2 us)
Sparse Core Ops, SparseCore 0:
  16.6 44.6 all-reduce.15
  113.3 39.0 all-reduce.17
  162.0 42.7 all-reduce.19
  310.4 43.6 all-reduce.35
  365.3 42.0 all-reduce.23
  415.9 42.6 all-reduce.21
  589.8 42.4 all-reduce.33
  646.2 42.0 all-reduce.25
  762.5 38.0 all-reduce.27
  806.6 41.8 all-reduce.29
  852.5 87.6 all-reduce.31
where the time goes:
time: 963 us; the launch traced here: 950 us
  waiting for transfers between devices  445 us (46%)
  local copies, waits for them, and re-layouts  132 us (14%)
  matrix products  95.4 us (10%)
  blocking collectives  95.1 us (10%)
  other arithmetic  83 us (9%)
  starting transfers between devices  82.3 us (9%)
  between operations  17 us (2%)
    psum x3, waiting for transfers between devices, layer_forward(): attended = lax.psum(partial_attn, 'head')  117 us
    psum x3, waiting for transfers between devices, layer_backward(): lax.psum(grad_normed_a.astype(jnp.bfloat16), 'head').astype(jnp.float32)  109 us
    psum x3, waiting for transfers between devices, layer_backward(): lax.psum(jnp.sum(grad_slot_rows, axis=1).astype(jnp.bfloat16), 'head')  105 us
    psum x1, blocking collectives, on_device(): lax.psum(table_part.astype(jnp.bfloat16), 'expert').astype(jnp.float32)  75.9 us
    psum x1, waiting for transfers between devices, layer_forward(): lax.psum(slot_part.astype(jnp.bfloat16), 'head').astype(jnp.float32)  38 us
    all_to_all x3, waiting for transfers between devices, layer_backward(): lax.all_to_all(row_buffer, 'expert', split_axis=0, concat_axis=1, tiled=T...  21.8 us
  transfers between devices with their start and end apart: 29, of which 26 were waited for; matrix products, arithmetic and copies ran while one was open for 16% of the time, Pallas kernels for 0%

commit v1 on v0

--- a/solution.py
+++ b/solution.py
@@ -136,7 +136,9 @@
     partial_attn, saved_attn = attend_forward(
         normed_a, proj_weight, out_weight, table, causal, onehot
     )
-    attended = lax.psum(partial_attn, "head")
+    attended = partial_attn
+    for hop in (1, 2):
+        attended = attended + lax.ppermute(attended, "head", [(dev, dev ^ hop) for dev in range(4)])
     middle = values + attended
     scale_m = norm_scale(middle)
     normed_m = (middle * scale_m * gain_m).astype(jnp.bfloat16)

time: 963 us -> 920 us (0.955)
  waiting for transfers between devices: 445 us -> 359 us
  other arithmetic: 83 us -> 101 us
  local copies, waits for them, and re-layouts: 132 us -> 149 us
  starting transfers between devices: 82.3 us -> 92 us
    psum x3 -> x0, waiting for transfers between devices: 117 us -> none  [layer_forward(): attended = lax.psum(partial_attn, 'head')]
    ppermute x0 -> x6, waiting for transfers between devices: none -> 29.4 us  [layer_forward(): lax.ppermute(attended, 'head', [(dev, dev ^ hop) for dev in range(4)])]
    ppermute x0 -> x6, starting transfers between devices: none -> 10.5 us  [layer_forward(): lax.ppermute(attended, 'head', [(dev, dev ^ hop) for dev in range(4)])]
  transfers between devices with their start and end apart: 29 -> 32, of which waited for: 26 -> 28; matrix products, arithmetic and copies ran while one was open for 16% -> 19% of each run, Pallas kernels for 0% -> 0%
where the time goes in v1:
time: 920 us; the launch traced here: 907 us
  waiting for transfers between devices  359 us (39%)
  local copies, waits for them, and re-layouts  149 us (16%)
  other arithmetic  101 us (11%)
  blocking collectives  97.1 us (11%)
  starting transfers between devices  92 us (10%)
  matrix products  91.2 us (10%)
  between operations  17.4 us (2%)
    psum x3, waiting for transfers between devices, layer_backward(): lax.psum(grad_normed_a.astype(jnp.bfloat16), 'head').astype(jnp.float32)  109 us
    psum x3, waiting for transfers between devices, layer_backward(): lax.psum(jnp.sum(grad_slot_rows, axis=1).astype(jnp.bfloat16), 'head')  106 us
    psum x1, blocking collectives, on_device(): lax.psum(table_part.astype(jnp.bfloat16), 'expert').astype(jnp.float32)  75.9 us
    psum x1, waiting for transfers between devices, layer_forward(): lax.psum(slot_part.astype(jnp.bfloat16), 'head').astype(jnp.float32)  38.2 us
    ppermute x6, waiting for transfers between devices, layer_forward(): lax.ppermute(attended, 'head', [(dev, dev ^ hop) for dev in range(4)])  29.4 us
    all_to_all x1, blocking collectives, layer_forward(): lax.all_to_all(buffer.reshape(experts, 1, capacity, width), 'expert', spl...  21.2 us
    all_to_all x3, waiting for transfers between devices, layer_backward(): lax.all_to_all(row_buffer, 'expert', split_axis=0, concat_axis=1, tiled=T...  20.1 us
    all_to_all x3, starting transfers between devices, layer_backward(): lax.all_to_all(row_buffer, 'expert', split_axis=0, concat_axis=1, tiled=T...  18.5 us
  transfers between devices with their start and end apart: 32, of which 28 were waited for; matrix products, arithmetic and copies ran while one was open for 19% of the time, Pallas kernels for 0%

profile of v1, /device:TPU:0, one launch (start us, length us, event | category | flops | bytes accessed | tf_op | source)
XLA Modules:
  0.0 907.3 jit_solution(13211765224380618005)
XLA Ops:
  45.5 3.6 collective-permute-done.1
  55.6 21.2 %all_to_all.189 = bf16[32,1,12,768]{3,2,1,0:T(8,128)(2,1)S(1)} all-to-all(bf16[32,1,12,768]{3,2,1,0:T(8,128)(2,1)} %bitcast.589), channel_id=1, replica_groups=mesh['section'=2,'expert'=16,'head'=4] {'expert'}, dimensions={0} | all-to-all | bytes 1179648 | tf_op jit(solution)/shard_map/all_to_all | solution.py:153
  77.8 3.8 fusion.44
  84.1 3.6 all-to-all-start.1
  88.1 10.0 %all-to-all-done.1 = bf16[2,16,12,768]{3,0,2,1:T(2,128)(2,1)S(1)} async-done(((bf16[2,16,12,768]{3,0,2,1:T(2,128)(2,1)}), bf16[2,16,12,768]{3,0,2,1:T(2,128)(2,1)S(1)}, u32[]{:S(2)}, u32[]{:S(2)}) %all-to-all-start.1) | async-done | bytes 589856 | tf_op jit(solution)/shard_map/all_to_all | solution.py:165
  106.0 38.2 %all-reduce.13.cloned.1.call-done = bf16[128,2,768]{2,1,0:T(2,128)(2,1)} async-done(((bf16[128,2,768]{2,1,0:T(2,128)(2,1)}), bf16[128,2,768]{2,1,0:T(2,128)(2,1)}) %all-reduce.13.cloned.1.call-update) | async-done | bytes 393232 | tf_op jit(solution)/shard_map/psum | solution.py:173
  153.4 10.9 %collective-permute-done.3 = f32[128,768]{1,0:T(8,128)S(1)} collective-permute-done((f32[128,768]{1,0:T(8,128)S(1)}, f32[128,768]{1,0:T(8,128)S(1)}, u32[]{:S(2)}, u32[]{:S(2)}) %collective-permute-start.3) | collective-permute-done | bytes 393248 | tf_op jit(solution)/shard_map/ppermute | solution.py:141
  166.7 9.8 %collective-permute-done.4 = f32[128,768]{1,0:T(8,128)S(1)} collective-permute-done((f32[128,768]{1,0:T(8,128)S(1)}, f32[128,768]{1,0:T(8,128)S(1)}, u32[]{:S(2)}, u32[]{:S(2)}) %collective-permute-start.4) | collective-permute-done | bytes 393248 | tf_op jit(solution)/shard_map/ppermute | solution.py:141
  184.6 7.0 all-to-all-start.7
  197.8 7.1 all-to-all-done.7
  204.9 4.3 all-to-all-start.2
  215.0 6.6 all-to-all-done.2
  221.6 4.7 all-to-all-start.6
  230.7 3.7 fusion.47
  238.2 6.0 all-to-all-start.3
  255.5 4.8 all-to-all-start.8
  285.8 36.5 %all-reduce.27.cloned.1.call-done = (bf16[128,768]{1,0:T(8,128)(2,1)}, bf16[128,2,768]{2,1,0:T(2,128)(2,1)}) async-done(((bf16[128,768]{1,0:T(8,128)(2,1)}, bf16[128,2,768]{2,1,0:T(2,128)(2,1)}), (bf16[128,768]{1,0:T(8,128)(2,1)}, bf16[128,2,768]{2,1,0:T(2,128)(2,1)})) %all-reduce.27.cloned.1.call-update) | async-done | bytes 589840 | tf_op jit(solution)/shard_map/psum | solution.py:246
  322.3 3.9 fusion.170
  339.5 38.3 %all-reduce.15.cloned.1.call-done = bf16[128,768]{1,0:T(8,128)(2,1)} async-done(((bf16[128,768]{1,0:T(8,128)(2,1)}), bf16[128,768]{1,0:T(8,128)(2,1)}) %all-reduce.15.cloned.1.call-update) | async-done | bytes 196624 | tf_op jit(solution)/shard_map/psum | solution.py:267
  385.7 3.0 fusion.217
  388.7 3.1 fusion.176
  416.6 7.2 all-to-all-start.13
  430.9 4.6 all-to-all-done.13
  435.5 4.3 all-to-all-start.4
  447.8 6.9 all-to-all-done.4
  454.6 4.3 all-to-all-start.10
  464.3 8.4 all-to-all-done.10
  472.7 4.7 all-to-all-start.9
  483.7 2.9 fusion.50
  490.2 7.3 all-to-all-start.5
  508.0 4.7 all-to-all-start.11
  512.9 3.1 fusion.212
  536.7 3.0 fusion.177
  539.7 38.6 %all-reduce.25.cloned.1.call-done = (bf16[128,768]{1,0:T(8,128)(2,1)}, bf16[128,2,768]{2,1,0:T(2,128)(2,1)}) async-done(((bf16[128,768]{1,0:T(8,128)(2,1)}, bf16[128,2,768]{2,1,0:T(2,128)(2,1)}), (bf16[128,768]{1,0:T(8,128)(2,1)}, bf16[128,2,768]{2,1,0:T(2,128)(2,1)})) %all-reduce.25.cloned.1.call-update) | async-done | bytes 589840 | tf_op jit(solution)/shard_map/psum | solution.py:246
  599.3 39.0 %all-reduce.17.cloned.1.call-done = bf16[128,768]{1,0:T(8,128)(2,1)} async-done(((bf16[128,768]{1,0:T(8,128)(2,1)}), bf16[128,768]{1,0:T(8,128)(2,1)}) %all-reduce.17.cloned.1.call-update) | async-done | bytes 196624 | tf_op jit(solution)/shard_map/psum | solution.py:267
  658.5 3.1 scatter_custom_fusion.5
  663.7 7.2 all-to-all-start.12
  674.2 11.6 %all-to-all-done.12 = bf16[32,1,12,768]{3,2,1,0:T(8,128)(2,1)} async-done(((bf16[32,1,12,768]{3,2,1,0:T(8,128)(2,1)}), bf16[32,1,12,768]{3,2,1,0:T(8,128)(2,1)}, u32[]{:S(2)}, u32[]{:S(2)}) %all-to-all-start.12) | async-done | bytes 589856 | tf_op jit(solution)/shard_map/all_to_all | solution.py:224
  688.0 3.1 fusion.74
  693.6 4.3 all-to-all-start.14
  698.1 7.2 add_bitcast_fusion
  705.4 4.2 all-to-all-done.14
  719.3 7.2 add_bitcast_fusion.1
  726.5 30.9 %all-reduce.19.cloned.1.call-done = bf16[128,768]{1,0:T(8,128)(2,1)} async-done(((bf16[128,768]{1,0:T(8,128)(2,1)}), bf16[128,768]{1,0:T(8,128)(2,1)}) %all-reduce.19.cloned.1.call-update) | async-done | bytes 196624 | tf_op jit(solution)/shard_map/psum | solution.py:246
  763.0 3.5 fusion.34
  773.2 31.7 %all-reduce.21.cloned.1.call-done = bf16[128,768]{1,0:T(8,128)(2,1)} async-done(((bf16[128,768]{1,0:T(8,128)(2,1)}), bf16[128,768]{1,0:T(8,128)(2,1)}) %all-reduce.21.cloned.1.call-update) | async-done | bytes 196624 | tf_op jit(solution)/shard_map/psum | solution.py:267
  807.3 75.9 %all-reduce = (bf16[1,3,32]{2,1,0:T(4,128)(2,1)}, bf16[1,768]{1,0:T(2,128)(2,1)}, bf16[1,768]{1,0:T(2,128)(2,1)S(1)}, bf16[1,768,32]{1,2,0:T(8,128)(2,1)}) all-reduce(bf16[1,3,32]{2,1,0:T(4,128)(2,1)} %fusion.153, bf16[1,768]{1,0:T(2,128)(2,1)S(1)} %broadcast_in_dim.93, ...), channel_id=1, replica_groups=mesh['section'=2,'expert'=16,'head'=4] {'expert'}, use_global_device_ids=true, to_apply=%region_75.76 | all-reduce | flops 26208 | bytes 104832 | tf_op jit(solution)/shard_map/psum | solution.py:344
  890.4 6.4 all-reduce.23.cloned.1.call-done
  (785 shorter events, 324.6 us)
Async XLA Ops:
  7.2 70.6 %copy-start = (bf16[1,2,768,768]{3,2,1,0:T(8,128)(2,1)S(1)}, bf16[1,2,768,768]{3,2,1,0:T(8,128)(2,1)}, u32[]{:S(2)}) copy-start(bf16[1,2,768,768]{3,2,1,0:T(8,128)(2,1)} %param.20) | copy-start | bytes 7077892
  15.3 19.7 %collective-permute-start = (f32[128,768]{1,0:T(8,128)S(1)}, f32[128,768]{1,0:T(8,128)}, u32[]{:S(2)}, u32[]{:S(2)}) collective-permute-start(f32[128,768]{1,0:T(8,128)S(1)} %fusion.272), channel_id=1, source_target_pairs={{0,1},{1,0},{2,3},{3,2},{4,5},{5,4},{6,7},{7,6},{8,9},{9,8},{10,11... | collective-permute-start | bytes 1179656 | tf_op jit(solution)/shard_map/ppermute | solution.py:141
  36.9 12.3 %collective-permute-start.1 = (f32[128,768]{1,0:T(8,128)}, f32[128,768]{1,0:T(8,128)S(1)}, u32[]{:S(2)}, u32[]{:S(2)}) collective-permute-start(f32[128,768]{1,0:T(8,128)} %add.454), channel_id=1, source_target_pairs={{0,2},{1,3},{2,0},{3,1},{4,6},{5,7},{6,4},{7,5},{8,10},{9,11},{10,... | collective-permute-start | bytes 1179656 | tf_op jit(solution)/shard_map/ppermute | solution.py:141
  84.1 14.0 %all-to-all-start.1 = ((bf16[2,16,12,768]{3,0,2,1:T(2,128)(2,1)}), bf16[2,16,12,768]{3,0,2,1:T(2,128)(2,1)S(1)}, u32[]{:S(2)}, u32[]{:S(2)}) async-start(bf16[2,16,12,768]{3,0,2,1:T(2,128)(2,1)} %bitcast.602), calls=%async_computation.1 | async-start | bytes 1179648 | tf_op jit(solution)/shard_map/all_to_all | solution.py:165
  87.7 56.6 %all-reduce.13.cloned.1.call-start = ((), (), s32[]{:S(2)}) async-start(), calls=%async_computation.15 | async-start | bytes 786432 | tf_op jit(solution)/shard_map/psum | solution.py:173
  106.0 44.8 %copy-start.2 = (bf16[1,3,768,192]{2,3,1,0:T(8,128)(2,1)S(1)}, bf16[1,3,768,192]{2,3,1,0:T(8,128)(2,1)}, u32[]{:S(2)}) copy-start(bf16[1,3,768,192]{2,3,1,0:T(8,128)(2,1)} %param.15) | copy-start | bytes 2654212
  147.5 2.5 collective-permute-start.2
  152.8 11.5 %collective-permute-start.3 = (f32[128,768]{1,0:T(8,128)S(1)}, f32[128,768]{1,0:T(8,128)S(1)}, u32[]{:S(2)}, u32[]{:S(2)}) collective-permute-start(f32[128,768]{1,0:T(8,128)S(1)} %fusion.270), channel_id=1, source_target_pairs={{0,1},{1,0},{2,3},{3,2},{4,5},{5,4},{6,7},{7,6},{8,9},{9,8},{10,11... | collective-permute-start | bytes 1179656 | tf_op jit(solution)/shard_map/ppermute | solution.py:141
  164.3 12.2 %collective-permute-start.4 = (f32[128,768]{1,0:T(8,128)S(1)}, f32[128,768]{1,0:T(8,128)S(1)}, u32[]{:S(2)}, u32[]{:S(2)}) collective-permute-start(f32[128,768]{1,0:T(8,128)S(1)} %add.465), channel_id=1, source_target_pairs={{0,2},{1,3},{2,0},{3,1},{4,6},{5,7},{6,4},{7,5},{8,10},{9,11},{10,... | collective-permute-start | bytes 1179656 | tf_op jit(solution)/shard_map/ppermute | solution.py:141
  184.6 20.3 %all-to-all-start.7 = ((bf16[32,1,12,768]{3,2,1,0:T(8,128)(2,1)}), bf16[32,1,12,768]{3,2,1,0:T(8,128)(2,1)}, u32[]{:S(2)}, u32[]{:S(2)}) async-start(bf16[32,1,12,768]{3,2,1,0:T(8,128)(2,1)} %bitcast.587), calls=%async_computation.7 | async-start | bytes 1572864 | tf_op jit(solution)/shard_map/all_to_all | solution.py:225
  204.9 16.7 %all-to-all-start.2 = ((bf16[32,1,12,768]{3,2,1,0:T(8,128)(2,1)}), bf16[32,1,12,768]{3,2,1,0:T(8,128)(2,1)}, u32[]{:S(2)}, u32[]{:S(2)}) async-start(bf16[32,1,12,768]{3,2,1,0:T(8,128)(2,1)} %bitcast.585), calls=%async_computation.2 | async-start | bytes 1572864 | tf_op jit(solution)/shard_map/all_to_all | solution.py:153
  221.6 16.6 %all-to-all-start.6 = ((bf16[32,1,12,768]{3,2,1,0:T(8,128)(2,1)}), bf16[32,1,12,768]{3,2,1,0:T(8,128)(2,1)}, u32[]{:S(2)}, u32[]{:S(2)}) async-start(bf16[32,1,12,768]{3,2,1,0:T(8,128)(2,1)} %bitcast.80), calls=%async_computation.6 | async-start | bytes 1572864 | tf_op jit(solution)/shard_map/all_to_all | solution.py:224
  238.2 16.5 %all-to-all-start.3 = ((bf16[2,16,12,768]{3,0,2,1:T(2,128)(2,1)}), bf16[2,16,12,768]{3,0,2,1:T(2,128)(2,1)S(1)}, u32[]{:S(2)}, u32[]{:S(2)}) async-start(bf16[2,16,12,768]{3,0,2,1:T(2,128)(2,1)} %bitcast.600), calls=%async_computation.3 | async-start | bytes 1179648 | tf_op jit(solution)/shard_map/all_to_all | solution.py:165
  255.5 15.3 %all-to-all-start.8 = ((bf16[2,16,12,768]{3,0,2,1:T(2,128)(2,1)}), bf16[2,16,12,768]{3,0,2,1:T(2,128)(2,1)S(1)}, u32[]{:S(2)}, u32[]{:S(2)}) async-start(bf16[2,16,12,768]{3,0,2,1:T(2,128)(2,1)} %bitcast.88), calls=%async_computation.8 | async-start | bytes 1179648 | tf_op jit(solution)/shard_map/all_to_all | solution.py:238
  260.3 62.0 %all-reduce.27.cloned.1.call-start = ((), (), s32[]{:S(2)}) async-start(), calls=%async_computation.22 | async-start | bytes 1179648 | tf_op jit(solution)/shard_map/psum | solution.py:246
  277.7 44.7 %copy-start.70 = (bf16[128,2,768]{2,1,0:T(2,128)(2,1)S(1)}, bf16[128,2,768]{2,1,0:T(2,128)(2,1)}, u32[]{:S(2)}) copy-start(bf16[128,2,768]{2,1,0:T(2,128)(2,1)} %all-reduce.13.cloned.1.call-done) | copy-start | bytes 1179652
  279.4 50.5 %copy-start.23 = (f32[128,768]{1,0:T(8,128)S(1)}, f32[128,768]{1,0:T(8,128)}, u32[]{:S(2)}) copy-start(f32[128,768]{1,0:T(8,128)} %copy-done.22) | copy-start | bytes 1179652
  279.4 50.5 %copy-start.26 = (f32[128,768]{1,0:T(8,128)S(1)}, f32[128,768]{1,0:T(8,128)}, u32[]{:S(2)}) copy-start(f32[128,768]{1,0:T(8,128)} %copy-done.25) | copy-start | bytes 1179652
  279.4 98.4 %all-reduce.15.cloned.1.call-start = ((), (), s32[]{:S(2)}) async-start(), calls=%async_computation.16 | async-start | bytes 393216 | tf_op jit(solution)/shard_map/psum | solution.py:267
  334.4 43.3 %copy-start.7 = (bf16[128,768]{1,0:T(8,128)(2,1)S(1)}, bf16[128,768]{1,0:T(8,128)(2,1)}, u32[]{:S(2)}) copy-start(bf16[128,768]{1,0:T(8,128)(2,1)} %copy-done.6) | copy-start | bytes 589828
  337.5 42.2 %collective-permute-start.5 = (bf16[128,768]{1,0:T(8,128)(2,1)}, bf16[128,768]{1,0:T(8,128)(2,1)}, u32[]{:S(2)}, u32[]{:S(2)}) collective-permute-start(bf16[128,768]{1,0:T(8,128)(2,1)} %get-tuple-element.84), channel_id=1, source_target_pairs={{0,64},{1,65},{2,66},{3,67},{4,68},{5,69},{6,70},{7,71},{8,72},{9,... | collective-permute-start | bytes 589832 | tf_op jit(solution)/shard_map/ppermute | solution.py:14
  385.2 8.9 collective-permute-start.6
  394.1 9.8 %collective-permute-start.7 = (f32[128,768]{1,0:T(8,128)S(1)}, f32[128,768]{1,0:T(8,128)}, u32[]{:S(2)}, u32[]{:S(2)}) collective-permute-start(f32[128,768]{1,0:T(8,128)S(1)} %add.476), channel_id=1, source_target_pairs={{0,2},{1,3},{2,0},{3,1},{4,6},{5,7},{6,4},{7,5},{8,10},{9,11},{10,... | collective-permute-start | bytes 1179656 | tf_op jit(solution)/shard_map/ppermute | solution.py:141
  416.6 18.8 %all-to-all-start.13 = ((bf16[32,1,12,768]{3,2,1,0:T(8,128)(2,1)}), bf16[32,1,12,768]{3,2,1,0:T(8,128)(2,1)}, u32[]{:S(2)}, u32[]{:S(2)}) async-start(bf16[32,1,12,768]{3,2,1,0:T(8,128)(2,1)} %bitcast.129), calls=%async_computation.13 | async-start | bytes 1572864 | tf_op jit(solution)/shard_map/all_to_all | solution.py:225
  425.9 15.2 %collective-permute-start.8 = (bf16[128,768]{1,0:T(8,128)(2,1)}, bf16[128,768]{1,0:T(8,128)(2,1)}, u32[]{:S(2)}, u32[]{:S(2)}) collective-permute-start(bf16[128,768]{1,0:T(8,128)(2,1)} %get-tuple-element.105), channel_id=1, source_target_pairs={{64,0},{65,1},{66,2},{67,3},{68,4},{69,5},{70,6},{71,7},{72,8},{73... | collective-permute-start | bytes 589832 | tf_op jit(solution)/shard_map/ppermute | solution.py:14
  435.5 19.2 %all-to-all-start.4 = ((bf16[32,1,12,768]{3,2,1,0:T(8,128)(2,1)}), bf16[32,1,12,768]{3,2,1,0:T(8,128)(2,1)}, u32[]{:S(2)}, u32[]{:S(2)}) async-start(bf16[32,1,12,768]{3,2,1,0:T(8,128)(2,1)} %bitcast.584), calls=%async_computation.4 | async-start | bytes 1572864 | tf_op jit(solution)/shard_map/all_to_all | solution.py:153
  454.6 18.0 %all-to-all-start.10 = ((bf16[32,1,12,768]{3,2,1,0:T(8,128)(2,1)}), bf16[32,1,12,768]{3,2,1,0:T(8,128)(2,1)}, u32[]{:S(2)}, u32[]{:S(2)}) async-start(bf16[32,1,12,768]{3,2,1,0:T(8,128)(2,1)} %bitcast.583), calls=%async_computation.10 | async-start | bytes 1572864 | tf_op jit(solution)/shard_map/all_to_all | solution.py:225
  472.7 17.5 %all-to-all-start.9 = ((bf16[32,1,12,768]{3,2,1,0:T(8,128)(2,1)}), bf16[32,1,12,768]{3,2,1,0:T(8,128)(2,1)}, u32[]{:S(2)}, u32[]{:S(2)}) async-start(bf16[32,1,12,768]{3,2,1,0:T(8,128)(2,1)} %bitcast.101), calls=%async_computation.9 | async-start | bytes 1572864 | tf_op jit(solution)/shard_map/all_to_all | solution.py:224
  490.2 17.8 %all-to-all-start.5 = ((bf16[2,16,12,768]{3,0,2,1:T(2,128)(2,1)}), bf16[2,16,12,768]{3,0,2,1:T(2,128)(2,1)}, u32[]{:S(2)}, u32[]{:S(2)}) async-start(bf16[2,16,12,768]{3,0,2,1:T(2,128)(2,1)} %bitcast.68), calls=%async_computation.5 | async-start | bytes 1179648 | tf_op jit(solution)/shard_map/all_to_all | solution.py:165
  508.0 15.2 %all-to-all-start.11 = ((bf16[2,16,12,768]{3,0,2,1:T(2,128)(2,1)}), bf16[2,16,12,768]{3,0,2,1:T(2,128)(2,1)}, u32[]{:S(2)}, u32[]{:S(2)}) async-start(bf16[2,16,12,768]{3,0,2,1:T(2,128)(2,1)} %bitcast.599), calls=%async_computation.11 | async-start | bytes 1179648 | tf_op jit(solution)/shard_map/all_to_all | solution.py:238
  512.7 65.7 %all-reduce.25.cloned.1.call-start = ((), (), s32[]{:S(2)}) async-start(), calls=%async_computation.21 | async-start | bytes 1179648 | tf_op jit(solution)/shard_map/psum | solution.py:246
  535.0 103.3 %all-reduce.17.cloned.1.call-start = ((), (), s32[]{:S(2)}) async-start(), calls=%async_computation.17 | async-start | bytes 393216 | tf_op jit(solution)/shard_map/psum | solution.py:267
  536.7 41.7 %copy-start.47 = (f32[128,768]{1,0:T(8,128)S(1)}, f32[128,768]{1,0:T(8,128)}, u32[]{:S(2)}) copy-start(f32[128,768]{1,0:T(8,128)} %copy-done.46) | copy-start | bytes 1179652
  539.7 44.7 %copy-start.27 = (f32[128,768]{1,0:T(8,128)S(1)}, f32[128,768]{1,0:T(8,128)}, u32[]{:S(2)}) copy-start(f32[128,768]{1,0:T(8,128)} %copy-done.25) | copy-start | bytes 1179652
  539.7 44.7 %copy-start.29 = (f32[128,768]{1,0:T(8,128)S(1)}, f32[128,768]{1,0:T(8,128)}, u32[]{:S(2)}) copy-start(f32[128,768]{1,0:T(8,128)} %copy-done.28) | copy-start | bytes 1179652
  596.1 42.3 %copy-start.205 = (f32[128]{0:T(128)S(1)}, f32[128]{0:T(128)}, u32[]{:S(2)}) copy-start(f32[128]{0:T(128)} %get-tuple-element.144) | copy-start | bytes 1540
  596.1 44.1 %copy-start.8 = (bf16[128,768]{1,0:T(8,128)(2,1)S(1)}, bf16[128,768]{1,0:T(8,128)(2,1)}, u32[]{:S(2)}) copy-start(bf16[128,768]{1,0:T(8,128)(2,1)} %copy-done.6) | copy-start | bytes 589828
  596.1 44.1 %copy-start.21 = (f32[128,768]{1,0:T(8,128)S(1)}, f32[128,768]{1,0:T(8,128)}, u32[]{:S(2)}) copy-start(f32[128,768]{1,0:T(8,128)} %copy-done.19) | copy-start | bytes 1179652
  596.1 44.1 %copy-start.193 = (f32[128]{0:T(128)S(1)}, f32[128]{0:T(128)}, u32[]{:S(2)}) copy-start(f32[128]{0:T(128)} %get-tuple-element.148) | copy-start | bytes 1540
  596.1 44.1 %copy-start.217 = (f32[128]{0:T(128)S(1)}, f32[128]{0:T(128)}, u32[]{:S(2)}) copy-start(f32[128]{0:T(128)} %copy-done.216) | copy-start | bytes 1540
  643.4 3.3 collective-permute-start.9
  663.7 22.2 %all-to-all-start.12 = ((bf16[32,1,12,768]{3,2,1,0:T(8,128)(2,1)}), bf16[32,1,12,768]{3,2,1,0:T(8,128)(2,1)}, u32[]{:S(2)}, u32[]{:S(2)}) async-start(bf16[32,1,12,768]{3,2,1,0:T(8,128)(2,1)} %bitcast.586), calls=%async_computation.12 | async-start | bytes 1572864 | tf_op jit(solution)/shard_map/all_to_all | solution.py:224
  693.6 16.0 %all-to-all-start.14 = ((bf16[2,16,12,768]{3,0,2,1:T(2,128)(2,1)}), bf16[2,16,12,768]{3,0,2,1:T(2,128)(2,1)}, u32[]{:S(2)}, u32[]{:S(2)}) async-start(bf16[2,16,12,768]{3,0,2,1:T(2,128)(2,1)} %bitcast.601), calls=%async_computation.14 | async-start | bytes 1179648 | tf_op jit(solution)/shard_map/all_to_all | solution.py:238
  697.8 59.6 %all-reduce.19.cloned.1.call-start = ((), (), s32[]{:S(2)}) async-start(), calls=%async_computation.18 | async-start | bytes 393216 | tf_op jit(solution)/shard_map/psum | solution.py:246
  719.3 85.6 %all-reduce.21.cloned.1.call-start = ((), (), s32[]{:S(2)}) async-start(), calls=%async_computation.19 | async-start | bytes 393216 | tf_op jit(solution)/shard_map/psum | solution.py:267
  762.9 133.9 %all-reduce.23.cloned.1.call-start = ((), (), s32[]{:S(2)}) async-start(), calls=%async_computation.20 | async-start | bytes 2359296 | tf_op jit(solution)/shard_map/psum | solution.py:342
  767.5 39.1 %copy-start.166 = (f32[768]{0:T(1024)S(1)}, f32[768]{0:T(1024)}, u32[]{:S(2)}) copy-start(f32[768]{0:T(1024)} %get-tuple-element.52) | copy-start | bytes 9220
  767.5 120.9 %copy-start.69 = (f32[128,768]{1,0:T(8,128)S(1)}, f32[128,768]{1,0:T(8,128)}, u32[]{:S(2)}) copy-start(f32[128,768]{1,0:T(8,128)} %copy-done.68) | copy-start | bytes 1179652
  (208 other events, 1316.2 us)
Sparse Core Ops, SparseCore 0:
  104.7 39.4 all-reduce.12
  279.5 42.7 all-reduce.26
  335.6 42.0 all-reduce.14
  535.1 43.2 all-reduce.24
  596.2 42.0 all-reduce.16
  719.3 38.0 all-reduce.18
  763.0 41.8 all-reduce.20
  809.2 87.5 all-reduce.22
